TPU v7x, 32 devices: a whole 2x2x4 slice. The times are simulated.
32 devices in a mesh: dp: 8 (over z, x), tensor: 4 (over y, core).
Axes of the slice: x: 2, y: 2, z: 4, core: 2. Of those that a mesh axis runs over, the one named last changes fastest.
Arguments:
- tokens: bfloat16 [8192, 1024], P(('dp', 'tensor')), may hold values from -24 to 24
- cotangent: bfloat16 [8192, 1024], P(('dp', 'tensor')), may hold values from -6 to 6
- bucket_start: int32 [32], replicated, may hold values from 0 to 30, as said below
- w_qkv: bfloat16 [1024, 3072], P(('dp', 'tensor')), may hold values from -0.1875 to 0.1875
- w_out: bfloat16 [1024, 1024], P(('dp', 'tensor')), may hold values from -0.1875 to 0.1875
- s_qk: bfloat16 [1024], P(('dp', 'tensor')), may hold values from 0.796875 to 1.59375
- alpha_a: bfloat16 [1024], P(('dp', 'tensor')), may hold values from 0.14941406 to 0.59765625
- alpha_m: bfloat16 [1024], P(('dp', 'tensor')), may hold values from 0.14941406 to 0.59765625
- w_up: bfloat16 [1024, 4096], P('dp', 'tensor'), may hold values from -0.1875 to 0.1875
- w_gate: bfloat16 [1024, 4096], P('dp', 'tensor'), may hold values from -0.1875 to 0.1875
- w_down: bfloat16 [1024, 4096], P('dp', 'tensor'), may hold values from -0.09375 to 0.09375
- s_u: bfloat16 [4096], P('tensor'), may hold values from 0.5 to 2
- s_v: bfloat16 [4096], P('tensor'), may hold values from 0.5 to 2
Outputs:
- layer_out: bfloat16 [8192, 1024], P(('dp', 'tensor'))
- grad_tokens: bfloat16 [8192, 1024], P(('dp', 'tensor'))
- grad_w_qkv: float32 [1024, 3072], P(('dp', 'tensor'))
- grad_w_out: float32 [1024, 1024], P(('dp', 'tensor'))
- grad_s_qk: float32 [1024], P(('dp', 'tensor'))
- grad_alpha_a: float32 [1024], P(('dp', 'tensor'))
- grad_alpha_m: float32 [1024], P(('dp', 'tensor'))
- grad_w_up: float32 [1024, 4096], P('dp', 'tensor')
- grad_w_gate: float32 [1024, 4096], P('dp', 'tensor')
- grad_w_down: float32 [1024, 4096], P('dp', 'tensor')
- grad_s_u: float32 [4096], P('tensor')
- grad_s_v: float32 [4096], P('tensor')
- stream_rms: float32 [3], replicated
Inputs may be any that keep to these rules, and one draw needn't show every extreme that they name: Buckets are the aligned runs of 256 token rows, and groups the aligned runs of 4 buckets. A sequence is either all 4 buckets of a group or two buckets 2i and 2i + 1 of one group; bucket_start names the first bucket of the sequence. Half of the 8 groups, rounded up, are each one sequence; the last group is always made of two-bucket sequences, and which of the others are whole changes with the seed.
All inputs are finite; a program needn't handle non-finite values.
Results may differ from a plain program's by a relative error of at most 0.018.
Values may be sent and summed in bfloat16 or wider, within the bound.
A program may use at most 192 MiB of HBM per device.

v0:
```python
import functools
import math

import jax
import jax.numpy as jnp
from jax import lax
from jax.experimental import pallas as pl
from jax.experimental.pallas import tpu as pltpu
from jax.sharding import PartitionSpec as P

HEAD_DIM = 64


EPSILON = 1e-06
MASKED_SCORE = -1e30


def rms_rows(value):
    return value * lax.rsqrt(jnp.mean(value * value, axis=-1, keepdims=True) + EPSILON)


def rms_back(upstream, normed, source):
    factor = lax.rsqrt(jnp.mean(source * source, axis=-1, keepdims=True) + EPSILON)
    return factor * (upstream - normed * jnp.mean(upstream * normed, axis=-1, keepdims=True))


def unit_heads(value):
    shaped = value.reshape(value.shape[0], -1, HEAD_DIM)
    factor = lax.rsqrt(jnp.sum(shaped * shaped, axis=-1, keepdims=True) + EPSILON)
    return ((shaped * factor).reshape(value.shape), factor)


def unit_back(upstream, normed, factor):
    upper_grad = upstream.reshape(normed.shape[0], -1, HEAD_DIM)
    normed_heads = normed.reshape(normed.shape[0], -1, HEAD_DIM)
    result = factor * (
        upper_grad - normed_heads * jnp.sum(upper_grad * normed_heads, axis=-1, keepdims=True)
    )
    return result.reshape(upstream.shape)


def block_span(total_rows, row_count):
    units = total_rows // row_count
    block_units = max(1, min(units, 512 // row_count))
    while units % block_units:
        block_units -= 1
    return row_count * block_units


def local(
    tokens,
    cotangent,
    bucket_start,
    w_qkv,
    w_out,
    s_qk,
    alpha_a,
    alpha_m,
    w_up,
    w_gate,
    w_down,
    s_u,
    s_v,
):
    row_count, model_width = tokens.shape
    head_count = model_width // HEAD_DIM
    score_scale = math.sqrt(HEAD_DIM)
    spread = lax.axis_size("tensor")
    group_rows = spread * row_count
    tensor_slot = lax.axis_index("tensor")
    qkv_full, out_full, gain_qk, mix_attn, mix_mlp = (
        lax.all_gather(w_qkv, ("dp", "tensor"), axis=0, tiled=True),
        lax.all_gather(w_out, ("dp", "tensor"), axis=0, tiled=True),
        lax.all_gather(s_qk, ("dp", "tensor"), axis=0, tiled=True),
        lax.all_gather(alpha_a, ("dp", "tensor"), axis=0, tiled=True),
        lax.all_gather(alpha_m, ("dp", "tensor"), axis=0, tiled=True),
    )
    up_full, gate_full, down_full = (
        lax.all_gather(w_up, "dp", axis=0, tiled=True),
        lax.all_gather(w_gate, "dp", axis=0, tiled=True),
        lax.all_gather(w_down, "dp", axis=0, tiled=True),
    )
    gain_qk = gain_qk.astype(jnp.float32)
    mix_attn = mix_attn.astype(jnp.float32)
    mix_mlp = mix_mlp.astype(jnp.float32)
    scale_up = s_u.astype(jnp.float32)
    scale_gate = s_v.astype(jnp.float32)
    starts = lax.dynamic_slice_in_dim(bucket_start, lax.axis_index("dp") * spread, spread)
    key_seq = jnp.repeat(starts, row_count)
    own_seq = starts[tensor_slot]
    query_pos = tensor_slot * row_count + jnp.arange(row_count, dtype=jnp.int32)

    def allowed(key_start, key_count):
        key_pos = key_start + jnp.arange(key_count, dtype=jnp.int32)
        seq_part = lax.dynamic_slice_in_dim(key_seq, key_start, key_count)
        return (key_pos[None, :] <= query_pos[:, None]) & (seq_part[None, :] == own_seq)

    inputs = tokens.astype(jnp.float32)
    qkv = jnp.dot(tokens, qkv_full, preferred_element_type=jnp.float32)
    q_unit, q_factor = unit_heads(qkv[:, :model_width])
    k_unit, k_factor = unit_heads(qkv[:, model_width : 2 * model_width])
    query_low = (q_unit * gain_qk).astype(jnp.bfloat16)
    keys_low = (k_unit * gain_qk).astype(jnp.bfloat16)
    values_low = qkv[:, 2 * model_width :].astype(jnp.bfloat16)
    query_heads = query_low.reshape(row_count, head_count, HEAD_DIM)
    key_all, value_all = (
        lax.all_gather(keys_low, "tensor", axis=0, tiled=True),
        lax.all_gather(values_low, "tensor", axis=0, tiled=True),
    )
    key_block = block_span(group_rows, row_count)
    blocks = group_rows // key_block

    def block_scores(key_source, key_start, key_count):
        key_part = lax.dynamic_slice_in_dim(key_source, key_start, key_count).reshape(
            key_count, head_count, HEAD_DIM
        )
        return (
            jnp.einsum("qhd,khd->hqk", query_heads, key_part, preferred_element_type=jnp.float32)
            * score_scale
        )

    def stat_step(state_pair, block_index):
        row_top, row_total = state_pair
        key_start = block_index * key_block
        allowed_keys = allowed(key_start, key_block)[None]
        masked = jnp.where(allowed_keys, block_scores(key_all, key_start, key_block), MASKED_SCORE)
        new_top = jnp.maximum(row_top, jnp.max(masked, axis=-1))
        fresh = jnp.where(allowed_keys, jnp.exp(masked - new_top[..., None]), 0.0)
        row_total = row_total * jnp.exp(row_top - new_top) + jnp.sum(fresh, axis=-1)
        return ((new_top, row_total), None)

    start_state = (
        jnp.full((head_count, row_count), MASKED_SCORE, jnp.float32),
        jnp.zeros((head_count, row_count), jnp.float32),
    )
    (row_top, row_total), _ = lax.scan(stat_step, start_state, jnp.arange(blocks))
    log_total = row_top + jnp.log(row_total)

    def probs_for(key_source, key_start, key_count):
        scores = block_scores(key_source, key_start, key_count)
        allowed_keys = allowed(key_start, key_count)[None]
        return jnp.where(allowed_keys, jnp.exp(scores - log_total[..., None]), 0.0)

    def value_part(value_source, key_start, key_count):
        return lax.dynamic_slice_in_dim(value_source, key_start, key_count).reshape(
            key_count, head_count, HEAD_DIM
        )

    def out_step(carry_sum, block_index):
        key_start = block_index * key_block
        attn_probs = probs_for(key_all, key_start, key_block).astype(jnp.bfloat16)
        term = jnp.einsum(
            "hqk,khd->qhd",
            attn_probs,
            value_part(value_all, key_start, key_block),
            preferred_element_type=jnp.float32,
        )
        return (carry_sum + term, None)

    attended, _ = lax.scan(
        out_step, jnp.zeros((row_count, head_count, HEAD_DIM), jnp.float32), jnp.arange(blocks)
    )
    attended_low = attended.reshape(row_count, model_width).astype(jnp.bfloat16)
    branch_a = jnp.dot(attended_low, out_full, preferred_element_type=jnp.float32)
    h_attn = rms_rows(branch_a)
    resid_one = inputs + mix_attn * (h_attn - inputs)
    hidden_one = rms_rows(resid_one)
    hidden_low = hidden_one.astype(jnp.bfloat16)
    rows_all = lax.all_gather(hidden_low, "tensor", axis=0, tiled=True)
    up_raw = jnp.dot(rows_all, up_full, preferred_element_type=jnp.float32)
    gate_raw = jnp.dot(rows_all, gate_full, preferred_element_type=jnp.float32)
    up_scaled = up_raw * scale_up
    gate_scaled = gate_raw * scale_gate
    gate_sigmoid = jax.nn.sigmoid(gate_scaled)
    silu_gate = gate_scaled * gate_sigmoid
    inner_low = (up_scaled * silu_gate).astype(jnp.bfloat16)
    branch_m = lax.psum_scatter(
        jnp.einsum("tf,df->td", inner_low, down_full, preferred_element_type=jnp.float32).astype(
            jnp.bfloat16
        ),
        "tensor",
        scatter_dimension=0,
        tiled=True,
    ).astype(jnp.float32)
    h_mlp = rms_rows(branch_m)
    resid_two = hidden_one + mix_mlp * (h_mlp - hidden_one)
    result = rms_rows(resid_two)
    partial_stats = jnp.stack(
        [jnp.sum(branch_a * branch_a), jnp.sum(branch_m * branch_m), jnp.sum(resid_two * resid_two)]
    )
    upstream = cotangent.astype(jnp.float32)
    d_resid_two = rms_back(upstream, result, resid_two)
    grad_mix_mlp = jnp.sum(d_resid_two * (h_mlp - hidden_one), axis=0)
    d_branch_m = rms_back(mix_mlp * d_resid_two, h_mlp, branch_m).astype(jnp.bfloat16)
    grads_all = lax.all_gather(d_branch_m, "tensor", axis=0, tiled=True)
    d_inner = jnp.dot(grads_all, down_full, preferred_element_type=jnp.float32)
    grad_up_scaled = d_inner * silu_gate
    grad_gate_scaled = (
        d_inner * up_scaled * gate_sigmoid * (1.0 + gate_scaled * (1.0 - gate_sigmoid))
    )
    grad_scale_up = jnp.sum(grad_up_scaled * up_raw, axis=0)
    grad_scale_gate = jnp.sum(grad_gate_scaled * gate_raw, axis=0)
    up_grad_low = (grad_up_scaled * scale_up).astype(jnp.bfloat16)
    gate_grad_low = (grad_gate_scaled * scale_gate).astype(jnp.bfloat16)
    grad_down = jnp.einsum("td,tf->df", grads_all, inner_low, preferred_element_type=jnp.float32)
    grad_up = jnp.einsum("td,tf->df", rows_all, up_grad_low, preferred_element_type=jnp.float32)
    grad_gate = jnp.einsum("td,tf->df", rows_all, gate_grad_low, preferred_element_type=jnp.float32)
    first = jnp.einsum("tf,df->td", up_grad_low, up_full, preferred_element_type=jnp.float32)
    d_hidden_one = (1.0 - mix_mlp) * d_resid_two + lax.psum_scatter(
        (
            first
            + jnp.einsum("tf,df->td", gate_grad_low, gate_full, preferred_element_type=jnp.float32)
        ).astype(jnp.bfloat16),
        "tensor",
        scatter_dimension=0,
        tiled=True,
    ).astype(jnp.float32)
    d_resid_one = rms_back(d_hidden_one, hidden_one, resid_one)
    grad_mix_attn = jnp.sum(d_resid_one * (h_attn - inputs), axis=0)
    d_branch_a = rms_back(mix_attn * d_resid_one, h_attn, branch_a).astype(jnp.bfloat16)
    grad_out = jnp.einsum("tc,td->cd", attended_low, d_branch_a, preferred_element_type=jnp.float32)
    d_attended = jnp.einsum(
        "td,cd->tc", d_branch_a, out_full, preferred_element_type=jnp.float32
    ).astype(jnp.bfloat16)
    d_heads = d_attended.reshape(row_count, head_count, HEAD_DIM)
    row_delta = jnp.sum(d_heads.astype(jnp.float32) * attended, axis=-1).T
    key_back, value_back = (
        lax.all_gather(keys_low, "tensor", axis=0, tiled=True),
        lax.all_gather(values_low, "tensor", axis=0, tiled=True),
    )

    def score_grads(key_start, key_count):
        attn_probs = probs_for(key_back, key_start, key_count)
        d_probs = jnp.einsum(
            "qhd,khd->hqk",
            d_heads,
            value_part(value_back, key_start, key_count),
            preferred_element_type=jnp.float32,
        )
        d_scores = (attn_probs * (d_probs - row_delta[..., None])).astype(jnp.bfloat16)
        return (attn_probs, d_scores)

    def query_step(carry_sum, block_index):
        key_start = block_index * key_block
        attn_probs, d_scores = score_grads(key_start, key_block)
        key_part = lax.dynamic_slice_in_dim(key_back, key_start, key_block).reshape(
            key_block, head_count, HEAD_DIM
        )
        return (
            carry_sum
            + jnp.einsum("hqk,khd->qhd", d_scores, key_part, preferred_element_type=jnp.float32),
            None,
        )

    d_query, _ = lax.scan(
        query_step, jnp.zeros((row_count, head_count, HEAD_DIM), jnp.float32), jnp.arange(blocks)
    )
    d_query = d_query.reshape(row_count, model_width) * score_scale
    part_rows = lax.axis_size("tensor") * row_count
    sub_block = block_span(part_rows, row_count)

    def one_block(block_index):
        begin = block_index * sub_block
        attn_probs, d_scores = score_grads(begin, sub_block)
        d_keys = (
            jnp.einsum("hqk,qhd->khd", d_scores, query_heads, preferred_element_type=jnp.float32)
            * score_scale
        )
        d_values = jnp.einsum(
            "hqk,qhd->khd",
            attn_probs.astype(jnp.bfloat16),
            d_heads,
            preferred_element_type=jnp.float32,
        )
        return jnp.concatenate(
            [d_keys.reshape(sub_block, model_width), d_values.reshape(sub_block, model_width)],
            axis=1,
        )

    block_terms = lax.map(one_block, jnp.arange(part_rows // sub_block))
    key_grads = lax.psum_scatter(
        block_terms.reshape(part_rows, 2 * model_width).astype(jnp.bfloat16),
        "tensor",
        scatter_dimension=0,
        tiled=True,
    ).astype(jnp.float32)
    d_keys_own = key_grads[:, :model_width]
    d_values_own = key_grads[:, model_width:]
    grad_gain = jnp.sum(d_query * q_unit + d_keys_own * k_unit, axis=0)
    d_qkv = jnp.concatenate(
        [
            unit_back(d_query * gain_qk, q_unit, q_factor),
            unit_back(d_keys_own * gain_qk, k_unit, k_factor),
            d_values_own,
        ],
        axis=1,
    ).astype(jnp.bfloat16)
    grad_qkv = jnp.einsum("tc,tf->cf", tokens, d_qkv, preferred_element_type=jnp.float32)
    d_tokens = (1.0 - mix_attn) * d_resid_one + jnp.einsum(
        "tf,cf->tc", d_qkv, qkv_full, preferred_element_type=jnp.float32
    )
    sum_qkv, sum_out, sum_gain, sum_mix_attn, sum_mix_mlp = (
        lax.psum_scatter(grad_qkv, ("dp", "tensor"), scatter_dimension=0, tiled=True),
        lax.psum_scatter(grad_out, ("dp", "tensor"), scatter_dimension=0, tiled=True),
        lax.psum_scatter(grad_gain, ("dp", "tensor"), scatter_dimension=0, tiled=True),
        lax.psum_scatter(grad_mix_attn, ("dp", "tensor"), scatter_dimension=0, tiled=True),
        lax.psum_scatter(grad_mix_mlp, ("dp", "tensor"), scatter_dimension=0, tiled=True),
    )
    sum_up, sum_gate, sum_down = (
        lax.psum_scatter(
            grad_up.astype(jnp.bfloat16), "dp", scatter_dimension=0, tiled=True
        ).astype(jnp.float32),
        lax.psum_scatter(
            grad_gate.astype(jnp.bfloat16), "dp", scatter_dimension=0, tiled=True
        ).astype(jnp.float32),
        lax.psum_scatter(
            grad_down.astype(jnp.bfloat16), "dp", scatter_dimension=0, tiled=True
        ).astype(jnp.float32),
    )
    sum_scale_up, sum_scale_gate = lax.psum((grad_scale_up, grad_scale_gate), "dp")
    stat_sums = lax.psum(partial_stats, ("dp", "tensor"))
    entry_count = row_count * model_width * lax.axis_size("dp") * spread
    stream_rms = jnp.sqrt(stat_sums / entry_count)
    return (
        result.astype(jnp.bfloat16),
        d_tokens.astype(jnp.bfloat16),
        sum_qkv,
        sum_out,
        sum_gain,
        sum_mix_attn,
        sum_mix_mlp,
        sum_up,
        sum_gate,
        sum_down,
        sum_scale_up,
        sum_scale_gate,
        stream_rms,
    )


MESH = pl.DeviceIdType.MESH
BF16 = jnp.bfloat16
F32 = jnp.float32
LOG2E = 1.4426950408889634
COPIES = 224
VMEM_BYTES = 63 * 2**20
CH = 32


def nn(left, right):
    return lax.dot_general(left, right, (((1,), (0,)), ((), ())), preferred_element_type=F32)


def nt(left, right):
    return lax.dot_general(left, right, (((1,), (1,)), ((), ())), preferred_element_type=F32)


def tn(left, right):
    return lax.dot_general(left, right, (((0,), (0,)), ((), ())), preferred_element_type=F32)


def flip(index, bits):
    bit = 1
    while bit <= bits:
        if bits & bit:
            index = index + bit - 2 * bit * lax.rem(lax.div(index, bit), 2)
        bit *= 2
    return index


def mixed(a, b):
    low = lax.rem(a, 2) + lax.rem(b, 2) - 2 * lax.rem(a, 2) * lax.rem(b, 2)
    high_a, high_b = lax.div(a, 2), lax.div(b, 2)
    return low + 2 * (high_a + high_b - 2 * high_a * high_b)


def mean_rows(value):
    return jnp.mean(value, axis=-1, keepdims=True)


def rows(start, count=256):
    return pl.ds(pl.multiple_of(start * count, count), count)


def block(r):
    return pl.ds(r * 256, 256)


def fused_kernel(
    tokens, cotangent, bucket_start, w_qkv, w_out, s_qk, alpha_a, alpha_m, w_up, w_gate, w_down, scale_u,
    scale_v,
    layer_hbm, tokens_hbm, qkv_hbm, out_hbm, up_hbm, gate_hbm, down_hbm, stats_out,
    layer_out, grad_tokens, grad_qkv, grad_out, grad_up, grad_gate, grad_down,
    tok, cot, wq, wo, wu, wg, wd, small, small_t, small_d, gains,
    raw, qkv, linv, att, ato, branch, hid, h1, ur, gr, inn,
    part, from_core3, from_core1, from_y,
    dr2, dr1, d_inner_f32, db, dba, dat, dao, dqkv, delta,
    gd, x_down, x_down_x, x_up, x_gate, x_qkv, x_out, z_down, z_down_x, z_up, z_gate, z_qkv, z_out,
    o_core3, o_core1, o_y, osum, q_sum, q_low, q_piece, stats, s_tensor, s_x, s_z,
    send_sem, recv_sem, local_sem,
):
    d = lax.axis_index("dp")
    t = lax.axis_index("tensor")
    z = lax.div(d, 2)
    inner = lax.rem(lax.div(z + 1, 2), 2) == 1
    core, ynb, diag = (d, flip(t, 1)), (d, flip(t, 2)), (d, flip(t, 3))
    tensor_peer = {1: core, 2: ynb, 3: diag}
    xnb = (flip(d, 1), t)
    z_peer = {m: (flip(d, m), t) for m in (2, 4, 6)}

    barrier = pltpu.get_barrier_semaphore()
    peers = [core, ynb, diag, xnb] + [z_peer[m] for m in (2, 4, 6)]
    for peer in peers:
        pl.semaphore_signal(barrier, inc=1, device_id=peer, device_id_type=MESH)

    issued = []
    used = [0]

    def number():
        used[0] += 1
        return used[0] - 1

    def describe(src, dst, peer, at, to):
        return pltpu.make_async_remote_copy(
            src_ref=src,
            dst_ref=dst,
            send_sem=send_sem.at[at],
            recv_sem=recv_sem.at[to],
            device_id=peer,
            device_id_type=MESH,
        )

    def send(src, dst, peer):
        at = number()
        copy = describe(src, dst, peer, at, at)
        copy.start()
        issued.append(copy)
        return copy

    waited = set()

    def sent(copy):
        if id(copy) not in waited:
            waited.add(id(copy))
            copy.wait_send()

    locals_ = []

    def bring(src, dst):
        copy = pltpu.make_async_copy(src, dst, local_sem.at[len(locals_)])
        copy.start()
        locals_.append(copy)
        return copy

    outer = jnp.logical_not(inner)

    class Gather:
        def __init__(self, src, view):
            self.src, self.view = src, view
            self.at6, self.relay_at = number(), number()

        def start_x(self):
            self.x = [send(self.src, self.view(d), xnb)]

        def start_far(self):
            self.z = {4: send(self.src, self.view(d), z_peer[4])}
            self.start_straight()

        def start_straight(self):
            self.straight = describe(self.src, self.view(d), z_peer[6], self.at6, self.at6)
            pl.when(inner)(self.straight.start)

        def start_near(self):
            self.z[2] = send(self.src, self.view(d), z_peer[2])

        def start_z(self):
            self.start_far()
            self.start_near()

        def hop(self):
            self.z[4].wait_recv()
            self.hand_on()

        def hand_on(self):
            shard = self.view(flip(d, 4))
            self.relay = describe(shard, shard, z_peer[2], self.relay_at, self.at6)
            pl.when(inner)(self.relay.start)

        def forward_one(self, m):
            if m == 2:
                self.z[2].wait_recv()
            if m == 6:
                self.straight.wait_recv()
            shard = self.view(flip(d, m))
            self.x.append(send(shard, shard, xnb))

        def forward(self):
            self.forward_one(2)
            self.hop()
            self.forward_one(4)
            self.forward_one(6)

        def finish(self):
            for copy in self.x:
                copy.wait_recv()

        def release(self):
            for copy in [*self.z.values(), *self.x]:
                sent(copy)
            for copy in (self.straight, self.relay):
                pl.when(inner)(copy.wait_send)

    class GatherPairs(Gather):
        def __init__(self, src, shard, pair):
            super().__init__(src, pair)
            self.shard = shard

        def start_x(self):
            self.x = [send(self.src, self.shard(d), xnb)]

        def start_far(self):
            self.x[0].wait_recv()
            self.src = self.view(d)
            self.z = {4: send(self.src, self.view(d), z_peer[4])}

        def hop(self):
            self.z[4].wait_recv()
            self.start_straight()
            self.hand_on()

    def rows_of(ref, count=128):
        return lambda index: ref.at[rows(index, count)]

    def pair_of(ref):
        return lambda index: ref.at[rows(lax.div(index, 2))]

    take_qkv = Gather(wq.at[:, rows(d, 128), :], lambda index: wq.at[:, rows(index, 128), :])
    take_small = Gather(small_d.at[:, rows(d, 128)], lambda index: small_d.at[:, rows(index, 128)])
    take_out = Gather(w_out, lambda index: wo.at[index, t])
    take_up = Gather(w_up, rows_of(wu))
    take_gate = Gather(w_gate, rows_of(wg))
    take_down = GatherPairs(w_down, rows_of(wd), pair_of(wd))

    piece = s_qk.shape[0]
    own_qkv = pl.ds(pl.multiple_of(d * 128 + t * 32, 32), 32)

    def qkv_cols(slot, pair, j):
        return pl.ds(pl.multiple_of(j * 1024 + slot * 256 + pair * 128, 128), 128)

    def qkv_place(pair, j):
        return wq.at[pair, own_qkv, j * 128 : j * 128 + 128]

    parts_of_qkv = [(pair, j) for pair in range(2) for j in range(3)]
    local_qkv = [
        bring(w_qkv.at[:, qkv_cols(t, pair, j)], qkv_place(pair, j)) for pair, j in parts_of_qkv
    ]
    local_tok = bring(tokens, tok.at[block(0)])
    local_rest = [
        bring(w_out, wo.at[d, t]),
        bring(w_up, wu.at[rows(d, 128)]),
        bring(w_gate, wg.at[rows(d, 128)]),
        bring(w_down, wd.at[rows(d, 128)]),
        bring(cotangent, cot),
    ]
    place = jnp.where(
        lax.broadcasted_iota(jnp.int32, (piece, 128), 1)
        == lax.broadcasted_iota(jnp.int32, (piece, 128), 0) + t * piece,
        1.0,
        0.0,
    ).astype(BF16)
    small_row = lax.broadcasted_iota(jnp.int32, (16, 128), 0)
    placed = jnp.zeros((16, 128), F32)
    for index, vector in enumerate((s_qk, alpha_a, alpha_m)):
        placed = jnp.where(small_row == index, nn(vector[...].reshape(1, piece), place), placed)
    small[...] = placed.astype(BF16)
    stats[...] = jnp.zeros_like(stats)
    gain_u = scale_u[...].astype(F32).reshape(1, 1024)
    gain_v = scale_v[...].astype(F32).reshape(1, 1024)
    pl.semaphore_wait(barrier, len(peers))

    small_sends = [send(small, small_t.at[r - 1], tensor_peer[r]) for r in (2, 3, 1)]
    qkv_sends = [
        send(w_qkv.at[:, qkv_cols(flip(t, r), pair, j)], qkv_place(pair, j), tensor_peer[r])
        for r in (2, 3, 1)
        for pair, j in parts_of_qkv
    ]
    take_out.start_z()
    take_down.start_x()
    take_out.start_x()
    take_up.start_x()
    for copy in small_sends:
        copy.wait_recv()
    small_d[:, rows(d, 128)] = small[...] + small_t[0] + small_t[1] + small_t[2]
    take_small.start_z()
    take_small.start_x()
    for copy in local_qkv:
        copy.wait()
    for copy in qkv_sends:
        copy.wait_recv()
    take_qkv.start_z()
    take_qkv.start_x()
    tok_y = send(tokens, tok.at[block(2)], ynb)
    tok_core = send(tokens, tok.at[block(1)], core)
    take_up.start_far()

    take_out.hop()
    take_small.hop()
    take_small.forward_one(4)
    take_small.forward_one(2)
    take_qkv.hop()
    take_qkv.forward_one(4)
    take_up.start_near()
    take_qkv.forward_one(2)
    take_small.forward_one(6)
    take_qkv.forward_one(6)
    take_out.forward_one(4)
    take_out.forward_one(2)
    take_out.forward_one(6)
    take_gate.start_far()
    tok_y.wait_recv()
    tok_diag = send(tok.at[block(2)], tok.at[block(3)], core)
    take_small.finish()
    gains[...] = small_d[...].astype(F32)
    take_qkv.finish()
    local_tok.wait()
    tok_core.wait_recv()
    tok_diag.wait_recv()

    def gain_pair(pair):
        gain = gains[0:1, pl.ds(pl.multiple_of(t * 256 + pair * 128, 128), 128)]
        return jnp.concatenate([gain, gain], axis=1)

    first_head = lax.broadcasted_iota(jnp.int32, (256, 128), 1) < HEAD_DIM
    same_head = jnp.where(
        lax.div(lax.broadcasted_iota(jnp.int32, (256, 256), 0), HEAD_DIM)
        == lax.div(lax.broadcasted_iota(jnp.int32, (256, 256), 1), HEAD_DIM),
        1.0,
        0.0,
    ).astype(BF16)

    def head_sum(value):
        high = value.astype(BF16)
        low = (value - high.astype(F32)).astype(BF16)
        return nn(high, same_head) + nn(low, same_head)

    def qkv_step(r, carry):
        at = rows(r)
        x = tok[at, :]
        for pair in range(2):
            y = nn(x, wq[pair])
            qk = y[:, :256]
            raw[pair, at, :] = qk
            factor = lax.rsqrt(head_sum(qk * qk) + EPSILON)
            qkv[pair, at, :256] = (qk * factor * gain_pair(pair)).astype(BF16)
            qkv[pair, at, 256:] = y[:, 256:].astype(BF16)
        return carry

    lax.fori_loop(0, 4, qkv_step, 0)

    take_out.finish()
    local_rest[0].wait()
    wo_y = send(wo.at[:, t], wo.at[:, t], ynb)
    wo_core = send(wo.at[:, t], wo.at[:, t], core)

    def true_rows(i):
        return rows(flip(t, i))

    whole = jnp.where(bucket_start[d * 4] == bucket_start[d * 4 + 2], 1.0, 0.0)
    row_id = lax.broadcasted_iota(jnp.int32, (256, 256), 0)
    col_id = lax.broadcasted_iota(jnp.int32, (256, 256), 1)
    exp_scale = math.sqrt(HEAD_DIM) * LOG2E

    def two_heads(value):
        zero = jnp.zeros_like(value)
        return jnp.concatenate(
            [jnp.where(first_head, value, zero), jnp.where(first_head, zero, value)], axis=0
        )

    def one_of_two(value):
        return jnp.where(first_head, value[:256], value[256:])

    causal = jnp.concatenate([col_id <= row_id] * 2, axis=0)

    def attend(i):
        at = true_rows(i)

        def head_step(pair, carry):
            q = two_heads(qkv[pair, at, 0:128])
            acc = jnp.zeros((512, 128), F32)
            weight = jnp.zeros((512, 1), F32)
            for j in range(i + 1):
                key_at = true_rows(j)
                e = jnp.exp2(nt(q, qkv[pair, key_at, 128:256]) * exp_scale)
                if j == i:
                    e = jnp.where(causal, e, 0.0)
                elif j // 2 != i // 2:
                    e = e * whole
                weight = weight + jnp.sum(e, axis=1, keepdims=True)
                acc = acc + nn(e.astype(BF16), qkv[pair, key_at, 256:384])
            inverse = 1.0 / weight
            lanes = rows(pair, 128)
            linv[at, lanes] = one_of_two(jnp.broadcast_to(inverse, (512, 128)))
            att[at, lanes] = one_of_two(acc * inverse).astype(BF16)
            return carry

        lax.fori_loop(0, 2, head_step, 0)

    attend(0)
    attend(1)
    take_up.hop()
    take_up.forward_one(4)
    take_gate.start_near()
    take_gate.start_x()
    take_up.forward_one(2)
    for copy in local_rest[1:]:
        copy.wait()
    take_down.start_far()
    attend(2)
    attend(3)

    att_sends = [send(att.at[block(r)], ato.at[t], tensor_peer[r]) for r in (2, 3, 1)]
    ato[t] = att[block(0), :]
    wo_y.wait_recv()
    wo_far = send(wo.at[:, flip(t, 2)], wo.at[:, flip(t, 2)], core)
    take_up.forward_one(6)
    for copy in att_sends:
        copy.wait_recv()
    wo_core.wait_recv()
    wo_far.wait_recv()

    def out_rows(slot, columns):
        return wo[2 * slot : 2 * slot + 2, :, :, columns].reshape(256, 256)

    def out_step(n, carry):
        at = rows(n)
        acc = nn(ato[0], out_rows(0, at))
        for slot in range(1, 4):
            acc = acc + nn(ato[slot], out_rows(slot, at))
        branch[:, at] = acc
        return carry

    lax.fori_loop(0, 4, out_step, 0)

    mix_a = gains[1:2, :]
    mix_m = gains[2:3, :]

    def add_stat(row, value):
        stats[row : row + 1, :] = stats[row : row + 1, :] + jnp.sum(value, axis=0, keepdims=True)

    def first_norm(at):
        x = tok[at, :].astype(F32)
        ba = branch[at, :]
        fa = lax.rsqrt(mean_rows(ba * ba) + EPSILON)
        ha = ba * fa
        r1 = x + mix_a * (ha - x)
        f1 = lax.rsqrt(mean_rows(r1 * r1) + EPSILON)
        return x, ba, fa, ha, f1, r1 * f1

    def norm_step(c, carry):
        at = rows(c, CH)
        _, ba, _, _, _, hidden = first_norm(at)
        add_stat(3, ba * ba)
        hid[at, :] = hidden
        h1[at, :] = hidden.astype(BF16)
        return carry

    lax.fori_loop(0, 256 // CH, norm_step, 0)

    def spread(ref):
        return send(ref.at[block(0)], ref.at[block(2)], ynb), send(
            ref.at[block(0)], ref.at[block(1)], core
        )

    def relay(ref, from_ynb):
        from_ynb.wait_recv()
        return send(ref.at[block(2)], ref.at[block(3)], core)

    h1_y, h1_core = spread(h1)
    take_gate.hop()
    take_gate.forward_one(4)
    take_down.start_near()
    take_gate.forward_one(2)
    h1_far = relay(h1, h1_y)
    take_gate.forward_one(6)
    take_down.hop()
    take_up.finish()
    h1_core.wait_recv()
    h1_far.wait_recv()
    take_gate.finish()

    def up_step(r, carry):
        at = rows(r)
        hidden = h1[at, :]
        u_raw = nn(hidden, wu[...])
        g_raw = nn(hidden, wg[...])
        gate = g_raw * gain_v
        silu = gate / (1.0 + jnp.exp(-gate))
        ur[at, :] = u_raw.astype(BF16)
        gr[at, :] = g_raw.astype(BF16)
        inn[at, :] = (u_raw * gain_u * silu).astype(BF16)
        return carry

    lax.fori_loop(0, 4, up_step, 0)

    class Reduce:
        def __init__(self, which, before, make):
            self.which, self.before, self.make = which, before, make
            self.copies = {}

        def run(self, order):
            for r in order:
                self.step(r)

        def step(self, r):
            k = self.which
            if r in self.before.copies:
                before = self.before.copies[r]
                for copy in before if isinstance(before, list) else [before]:
                    sent(copy)
            self.make(r)
            if r == 3:
                self.copies[3] = send(part.at[block(3)], from_core3.at[k], core)
            elif r == 2:
                self.copies[3].wait_recv()
                part[block(2), :] = (
                    part[block(2), :].astype(F32) + from_core3[k].astype(F32)
                ).astype(BF16)
                self.copies[2] = send(part.at[block(2)], from_y.at[k], ynb)
            elif r == 1:
                self.copies[1] = send(part.at[block(1)], from_core1.at[k], core)

        def finish(self):
            self.copies[1].wait_recv()
            self.copies[2].wait_recv()

        def at(self, where):
            k = self.which
            return (
                part[where, :].astype(F32)
                + from_core1[k, where, :].astype(F32)
                + from_y[k, where, :].astype(F32)
            )

    class ReduceColumns:
        def __init__(self):
            self.copies = {r: [] for r in (1, 2, 3)}
            self.columns = []

        def step(self, k):
            cols = rows(lax.div(flip(d, 2 * k), 2))
            part[:, cols] = nt(inn[...], wd[cols, :]).astype(BF16)
            self.columns.append(cols)
            self.copies[3].append(send(part.at[block(3), cols], from_core3.at[0, :, cols], core))
            self.copies[1].append(send(part.at[block(1), cols], from_core1.at[0, :, cols], core))

        def pass_on(self):
            done = len(self.copies[2])
            cols = self.columns[done]
            self.copies[3][done].wait_recv()
            part[block(2), cols] = (
                part[block(2), cols].astype(F32) + from_core3[0, :, cols].astype(F32)
            ).astype(BF16)
            self.copies[2].append(send(part.at[block(2), cols], from_y.at[0, :, cols], ynb))

        def finish(self):
            for r in (1, 2):
                for copy in self.copies[r]:
                    copy.wait_recv()

        at = Reduce.at
        which = 0

    sum_m = ReduceColumns()
    sum_m.step(0)
    take_down.z[2].wait_recv()
    sum_m.step(1)
    sum_m.pass_on()
    sum_m.step(2)
    sum_m.pass_on()
    take_down.straight.wait_recv()
    sum_m.step(3)
    sum_m.pass_on()
    sum_m.pass_on()
    sum_m.finish()

    def loss_step(c, carry):
        at = rows(c, CH)
        bm = sum_m.at(at)
        hidden = hid[at, :]
        fm = lax.rsqrt(mean_rows(bm * bm) + EPSILON)
        hm = bm * fm
        r2 = hidden + mix_m * (hm - hidden)
        f2 = lax.rsqrt(mean_rows(r2 * r2) + EPSILON)
        result = r2 * f2
        layer_out[at, :] = result.astype(BF16)
        up = cot[at, :].astype(F32)
        grad = f2 * (up - result * mean_rows(up * result))
        dr2[at, :] = grad
        add_stat(1, grad * (hm - hidden))
        add_stat(4, bm * bm)
        add_stat(5, r2 * r2)
        c_m = mix_m * grad
        db[at, :] = (fm * (c_m - hm * mean_rows(c_m * hm))).astype(BF16)
        return carry

    class Spread:
        def __init__(self, ref):
            self.ref, self.y, self.core = ref, [], []

        def piece(self, r, c):
            return self.ref.at[pl.ds(r * 256 + c * 64, 64)]

        def start(self, c):
            self.y.append(send(self.piece(0, c), self.piece(2, c), ynb))
            self.core.append(send(self.piece(0, c), self.piece(1, c), core))

        def relay(self, c):
            self.y[c].wait_recv()
            self.core.append(send(self.piece(2, c), self.piece(3, c), core))

    db_rows = Spread(db)
    for c in range(4):
        lax.fori_loop(c * (64 // CH), (c + 1) * (64 // CH), loss_step, 0)
        db_rows.start(c)

    class AlongZ:
        def __init__(self, view, landing):
            self.view, self.landing = view, landing
            self.at6, self.relay_at = number(), number()
            self.z = {}

        def far_copies(self):
            shard = self.view(flip(d, 6))
            return (
                describe(shard, self.landing.at[2], z_peer[6], self.at6, self.at6),
                describe(shard, self.landing.at[3], z_peer[2], self.relay_at, self.relay_at),
            )

        def start_far(self):
            straight, over = self.far_copies()
            pl.when(inner)(straight.start)
            pl.when(outer)(over.start)

        def push(self, k):
            shard = self.view(flip(d, 2 * k))
            if k == 3:
                self.start_far()
                self.straight, self.relay = self.far_copies()
            elif k == 2:

                @pl.when(inner)
                def _():
                    self.relay.wait_recv()
                    shard[...] = (shard[...].astype(F32) + self.landing[3].astype(F32)).astype(BF16)

                self.z[2] = send(shard, self.landing.at[1], z_peer[4])
            else:
                self.z[1] = send(shard, self.landing.at[0], z_peer[2])

        def total_into(self, out):
            self.z[1].wait_recv()
            self.z[2].wait_recv()
            out[...] = (
                self.view(d)[...].astype(F32)
                + self.landing[0].astype(F32)
                + self.landing[1].astype(F32)
            ).astype(out.dtype)

            @pl.when(inner)
            def _():
                self.straight.wait_recv()
                out[...] = (out[...].astype(F32) + self.landing[2].astype(F32)).astype(out.dtype)

        def settle(self):
            pl.when(inner)(self.straight.wait_send)
            pl.when(outer)(self.relay.wait_send)

    class Scatter(AlongZ):
        def __init__(self, view, from_x, landing):
            super().__init__(view, landing)
            self.from_x = from_x
            self.x = {}

        def ship(self, k):
            self.x[k] = send(self.view(flip(d, 2 * k + 1)), self.from_x.at[k], xnb)

        def ship_as_made(self, make, also=None):
            numbers = [number() for _ in range(4)]

            def copy_of(k, shard):
                at = numbers[0] + k
                return describe(self.view(shard), self.from_x.at[k], xnb, at, at)

            def step(n, carry):
                k = (7 - 2 * n + n // 2) % 4
                pair = mixed(z, k)
                make(rows(pair))
                copy_of(k, 2 * pair + 1 - lax.rem(d, 2)).start()
                if also is not None:
                    pl.when(n == 0)(also)
                return carry

            lax.fori_loop(0, 4, step, 0)
            for k in range(4):
                self.x[k] = copy_of(k, flip(d, 2 * k + 1))
                issued.append(self.x[k])

        def fold(self, k):
            self.x[k].wait_recv()
            own = self.view(flip(d, 2 * k))
            own[...] = (own[...].astype(F32) + self.from_x[k].astype(F32)).astype(BF16)
            if k in (1, 3):
                self.push(k)

    def weight_grad(left, right, out, scatter, also=None):
        def make(at):
            out[at, :] = tn(left[:, at], right[...]).astype(BF16)

        scatter.ship_as_made(make, also)

    def make_hidden(r):
        at = block(r)
        d_inner_f32[...] = nn(db[at, :], wd[...])

        def inner_step(c, carry):
            here = rows(c, CH)
            where = pl.ds(pl.multiple_of(r * 256 + c * CH, CH), CH)
            d_inner = d_inner_f32[here, :]
            u_raw = ur[where, :].astype(F32)
            g_raw = gr[where, :].astype(F32)
            gate = g_raw * gain_v
            sig = 1.0 / (1.0 + jnp.exp(-gate))
            up = u_raw * gain_u
            d_up = d_inner * (gate * sig)
            d_gate = d_inner * up * (sig * (1.0 + gate * (1.0 - sig)))
            add_stat(6, d_up * u_raw)
            add_stat(7, d_gate * g_raw)
            ur[where, :] = (d_up * gain_u).astype(BF16)
            gr[where, :] = (d_gate * gain_v).astype(BF16)
            return carry

        lax.fori_loop(0, 256 // CH, inner_step, 0)
        part[at, :] = (nt(ur[at, :], wu[...]) + nt(gr[at, :], wg[...])).astype(BF16)

    sum_h = Reduce(1, sum_m, make_hidden)
    for copy in db_rows.core[:4]:
        copy.wait_recv()
    sum_h.step(1)
    db_rows.relay(0)
    db_rows.relay(1)
    sum_h.step(0)
    db_rows.relay(2)
    db_rows.relay(3)
    for copy in db_rows.core[4:]:
        copy.wait_recv()
    half = slice(0, 512), slice(512, 1024)

    def down_pair(index):
        return gd.at[rows(lax.div(index, 2)), half[0]]

    def down_shard(index):
        return gd.at[rows(index, 128), half[1]]

    sum_down = AlongZ(down_pair, z_down)
    sum_down_x = Scatter(down_shard, x_down_x, z_down_x)

    weight_grad(db, inn, gd, sum_down_x, sum_down.start_far)
    sum_down.straight, sum_down.relay = sum_down.far_copies()
    sum_h.run((3, 2))

    gu, gg, go = wd, wu, wg
    for gather in (take_down, take_up, take_gate):
        gather.release()
    sum_up = Scatter(rows_of(gu), x_up, z_up)
    sum_gate = Scatter(rows_of(gg), x_gate, z_gate)
    weight_grad(h1, ur, gu, sum_up)
    sum_down.push(2)
    sum_down.push(1)
    weight_grad(h1, gr, gg, sum_gate)
    sum_down_x.fold(3)
    sum_down_x.fold(1)
    sum_h.finish()

    def mid_step(c, carry):
        at = rows(c, CH)
        x, _, fa, ha, f1, hidden = first_norm(at)
        d_hidden = (1.0 - mix_m) * dr2[at, :] + sum_h.at(at)
        grad = f1 * (d_hidden - hidden * mean_rows(d_hidden * hidden))
        dr1[at, :] = grad
        add_stat(0, grad * (ha - x))
        c_a = mix_a * grad
        dba[at, :] = (fa * (c_a - ha * mean_rows(c_a * ha))).astype(BF16)
        return carry

    lax.fori_loop(0, 256 // CH, mid_step, 0)

    dat_sends = []
    for r in (2, 3, 1, 0):
        slot = flip(t, r)
        weight = wo[pl.ds(2 * slot, 2)].reshape(256, 1024)
        value = nt(dba[...], weight).astype(BF16)
        if r:
            dat[r - 1] = value
            dat_sends.append(send(dat.at[r - 1], dao.at[block(r)], tensor_peer[r]))
        else:
            dao[block(0), :] = value
    for slot in range(4):
        g = tn(ato[slot], dba[...]).astype(BF16)
        for q in range(8):
            start = (q % 4) * 256 + (2 * slot + q // 4) * 32
            go[start : start + 32, :] = g[q * 32 : (q + 1) * 32, :]

    def go_rows(r):
        return rows(flip(t, r))

    go_core3 = send(go.at[go_rows(3)], o_core3, core)
    go_core1 = send(go.at[go_rows(1)], o_core1, core)
    sum_down_x.fold(2)
    sum_down_x.push(2)
    sum_down_x.fold(0)
    sum_up.fold(3)
    sum_up.fold(1)
    go_core3.wait_recv()
    go[go_rows(2), :] = (go[go_rows(2), :].astype(F32) + o_core3[...].astype(F32)).astype(BF16)
    go_y = send(go.at[go_rows(2)], o_y, ynb)

    head_rows = jnp.where(
        lax.broadcasted_iota(jnp.int32, (8, 256), 0)
        == lax.div(lax.broadcasted_iota(jnp.int32, (8, 256), 1), HEAD_DIM),
        1.0,
        0.0,
    ).astype(BF16)
    for copy in att_sends:
        sent(copy)

    def ready_step(r, carry):
        at = rows(r)
        scaled = (dao[at, :].astype(F32) * linv[at, :]).astype(BF16)
        dao[at, :] = scaled
        product = scaled.astype(F32) * att[at, :].astype(F32)
        high = product.astype(BF16)
        low = (product - high.astype(F32)).astype(BF16)
        delta[r] = nt(head_rows, high) + nt(head_rows, low)
        return carry

    key_grads, query_grads = branch, hid
    seen = jnp.concatenate([row_id <= col_id] * 2, axis=1)

    def lanes_of(r, half=0):
        return pl.ds(pl.multiple_of(r * 128 + half * 512, 128), 128)

    def attend_back(pair, query_r, key_r, visible):
        query_at, key_at = rows(query_r), rows(key_r)
        q = two_heads(qkv[pair, query_at, 0:128])
        do = two_heads(dao[query_at, pair * 128 : pair * 128 + 128])
        keys = qkv[pair, key_at, 128:256]
        e = visible(jnp.exp2(nt(keys, q) * exp_scale))
        d_prob = nt(qkv[pair, key_at, 256:384], do)
        shift = jnp.concatenate(
            [delta[query_r, 2 * pair + h : 2 * pair + h + 1, :] for h in range(2)], axis=1
        )
        d_score = (e * (d_prob - shift)).astype(BF16)
        key_grads[:, lanes_of(key_r)] += nn(d_score, q)
        key_grads[:, lanes_of(key_r, 1)] += nn(e.astype(BF16), do)
        query_grads[:, lanes_of(query_r)] += one_of_two(tn(d_score, keys))

    def diagonal(pair):
        def diagonal_step(r, carry):
            attend_back(pair, r, r, lambda e: jnp.where(seen, e, 0.0))
            return carry

        return diagonal_step

    def below(pair):
        def below_step(n, carry):
            i = 1 + lax.div(n, 3) + lax.div(n + 4, 5)
            j = n - lax.div(i * (i - 1), 2)
            apart = (lax.div(i, 2) - lax.div(j, 2)).astype(F32)
            factor = 1.0 - apart + apart * whole
            attend_back(pair, mixed(i, t), mixed(j, t), lambda e: e * factor)
            return carry

        return below_step

    def clear():
        key_grads[...] = jnp.zeros_like(key_grads)
        query_grads[...] = jnp.zeros_like(query_grads)

    def qkv_back(pair):
        scale = math.sqrt(HEAD_DIM)
        gain = gain_pair(pair)
        column = pl.ds(pl.multiple_of(t * 256 + pair * 128, 128), 128)

        def back_qkv_step(r, carry):
            at = rows(r)
            y = raw[pair, at, :]
            factor = lax.rsqrt(head_sum(y * y) + EPSILON)
            w = y * factor
            grad = (
                jnp.concatenate([query_grads[:, lanes_of(r)], key_grads[:, lanes_of(r)]], axis=1)
                * scale
            )
            both = jnp.sum(grad * w, axis=0, keepdims=True)
            stats[2:3, column] = stats[2:3, column] + both[:, :128] + both[:, 128:]
            c = grad * gain
            dqkv[pair, at, :256] = (factor * (c - w * head_sum(c * w))).astype(BF16)
            dqkv[pair, at, 256:] = key_grads[:, lanes_of(r, 1)].astype(BF16)
            return carry

        lax.fori_loop(0, 4, back_qkv_step, 0)

    gq = qkv

    def qkv_shard(pair):
        return lambda index: gq.at[pair, rows(index, 128), :]

    sum_qkv = [Scatter(qkv_shard(pair), x_qkv.at[pair], z_qkv.at[pair]) for pair in range(2)]

    def qkv_weight(pair):
        def make(at):
            gq[pair, at, :] = tn(tok[:, at], dqkv[pair]).astype(BF16)

        sum_qkv[pair].ship_as_made(make)

    clear()
    dat_sends[2].wait_recv()
    lax.fori_loop(0, 2, ready_step, 0)
    lax.fori_loop(0, 2, diagonal(0), 0)
    sum_up.fold(2)
    dat_sends[0].wait_recv()
    dat_sends[1].wait_recv()
    lax.fori_loop(2, 4, ready_step, 0)
    lax.fori_loop(2, 4, diagonal(0), 0)
    sum_up.push(2)
    sum_up.fold(0)
    lax.fori_loop(0, 6, below(0), 0)
    qkv_back(0)
    qkv_weight(0)
    clear()
    go_core1.wait_recv()
    go_y.wait_recv()
    osum[...] = (
        go[go_rows(0), :].astype(F32) + o_core1[...].astype(F32) + o_y[...].astype(F32)
    ).astype(BF16)
    sum_out = Scatter(rows_of(osum, 32), x_out, z_out)
    for k in (3, 1, 2, 0):
        sum_out.ship(k)
    sum_gate.fold(3)
    sum_gate.fold(1)
    lax.fori_loop(0, 4, diagonal(1), 0)
    sum_gate.fold(2)
    sum_gate.push(2)
    lax.fori_loop(0, 6, below(1), 0)
    qkv_back(1)
    qkv_weight(1)
    sum_gate.fold(0)
    sum_down.total_into(down_pair(d))
    down_x = send(gd.at[rows(flip(d, 1), 128), half[0]], x_down, xnb)

    small_back = [send(stats, s_tensor.at[r - 1], tensor_peer[r]) for r in (1, 2, 3)]

    def make_tokens(r):
        part[block(r), :] = (
            nt(dqkv[0, block(r), :], wq[0]) + nt(dqkv[1, block(r), :], wq[1])
        ).astype(BF16)

    sum_t = Reduce(2, sum_h, make_tokens)
    sum_t.run((3, 2))
    for k in (3, 1, 0, 2):
        sum_qkv[0].fold(k)
    sum_t.run((1, 0))
    sum_qkv[0].push(2)
    for k in (3, 1, 2, 0):
        sum_out.fold(k)
    sum_out.push(2)
    for copy in small_back:
        copy.wait_recv()
    over_tensor = s_tensor[0] + s_tensor[1] + s_tensor[2]
    shared = lax.broadcasted_iota(jnp.int32, (8, 1024), 0) < 6
    s_x[0] = stats[...] + jnp.where(shared, over_tensor, 0.0)
    stat_x = send(s_x.at[0], s_x.at[1], xnb)
    for k in (3, 1, 0, 2):
        sum_qkv[1].fold(k)
    sum_qkv[1].push(2)

    outgoing = []

    def put(src, dst):
        outgoing.append(bring(src, dst))

    put(layer_out, layer_hbm)
    down_x.wait_recv()
    grad_down[:, half[0]] = gd[rows(d, 128), half[0]].astype(F32) + x_down[...].astype(F32)
    sum_down_x.total_into(grad_down.at[:, half[1]])
    put(grad_down, down_hbm)
    sum_up.total_into(grad_up)
    put(grad_up, up_hbm)
    sum_gate.total_into(grad_gate)
    put(grad_gate, gate_hbm)
    sum_out.total_into(grad_out)
    put(grad_out, out_hbm)
    stat_x.wait_recv()
    s_z[0] = s_x[0] + s_x[1]
    stat_z = [send(s_z.at[0], s_z.at[k], z_peer[2 * k]) for k in (1, 2, 3)]
    for pair in range(2):
        sum_qkv[pair].total_into(q_sum.at[pair])
    q_low[...] = q_sum[...].astype(BF16)
    q_sends = [
        send(q_low.at[:, rows(flip(t, r), 32), :], q_piece.at[t], tensor_peer[r]) for r in (2, 3, 1)
    ]
    q_piece[t] = q_low[:, rows(t, 32), :]
    sum_t.finish()

    def last_step(c, carry):
        at = rows(c, CH)
        grad_tokens[at, :] = ((1.0 - mix_a) * dr1[at, :] + sum_t.at(at)).astype(BF16)
        return carry

    lax.fori_loop(0, 256 // CH, last_step, 0)
    put(grad_tokens, tokens_hbm)
    for copy in stat_z:
        copy.wait_recv()
    stats_out[...] = s_z[0] + s_z[1] + s_z[2] + s_z[3]
    for copy in q_sends:
        copy.wait_recv()
    for slot in range(4):
        for pair, j in parts_of_qkv:
            start = j * 1024 + slot * 256 + pair * 128
            grad_qkv[:, start : start + 128] = q_piece[
                slot, pair, :, j * 128 : j * 128 + 128
            ].astype(F32)
    put(grad_qkv, qkv_hbm)
    for gather in (take_qkv, take_small, take_out):
        gather.release()
    for scatter in (sum_down, sum_down_x, sum_up, sum_gate, sum_out, *sum_qkv):
        scatter.settle()
    for copy in issued:
        sent(copy)
    for copy in outgoing:
        copy.wait()


def finish_kernel(entries, *refs):
    large, stats, outs, held, sems = refs[:7], refs[7], refs[8:21], refs[21:28], refs[28]
    taken = [pltpu.make_async_copy(large[i], held[i], sems.at[0, i]) for i in range(7)]
    given = [pltpu.make_async_copy(held[i], outs[i], sems.at[1, i]) for i in range(7)]
    for copy in taken:
        copy.start()
    s_qk, alpha_a, alpha_m, s_u, s_v, stream = outs[7:]
    index = lax.axis_index("dp") * lax.axis_size("tensor") + lax.axis_index("tensor")
    piece = s_qk.shape[0]
    pick = lax.broadcasted_iota(jnp.int32, (1024, piece), 0) == (
        lax.broadcasted_iota(jnp.int32, (1024, piece), 1) + index * piece
    )
    own = lax.dot_general(
        stats[0:3, :],
        jnp.where(pick, 1.0, 0.0),
        (((1,), (0,)), ((), ())),
        precision=lax.Precision.HIGHEST,
        preferred_element_type=F32,
    )
    for ref, row in ((alpha_a, 0), (alpha_m, 1), (s_qk, 2)):
        ref[...] = own[row]
    s_u[...] = stats[6, :]
    s_v[...] = stats[7, :]
    stream[...] = jnp.sqrt(jnp.sum(stats[3:6, :], axis=1) / entries)
    for i in range(7):
        taken[i].wait()
        given[i].start()
    for copy in given:
        copy.wait()


def fits(mesh):
    return dict(mesh.shape) == {"dp": 8, "tensor": 4}


def fused(
    tokens, cotangent, bucket_start, w_qkv, w_out, s_qk, alpha_a, alpha_m, w_up, w_gate, w_down, s_u, s_v
):
    n_rows, width = tokens.shape
    piece = s_qk.shape[0]
    vmem = pl.BlockSpec(memory_space=pltpu.VMEM)
    smem = pl.BlockSpec(memory_space=pltpu.SMEM)
    hbm = pl.BlockSpec(memory_space=pl.ANY)
    bf = lambda *shape: pltpu.VMEM(shape, BF16)
    fl = lambda *shape: pltpu.VMEM(shape, F32)
    large = [
        jax.ShapeDtypeStruct(shape, kind)
        for shape, kind in (
            ((256, 1024), BF16), ((256, 1024), BF16), ((32, 3072), F32), ((32, 1024), F32),
            ((128, 1024), F32), ((128, 1024), F32), ((128, 1024), F32),
        )
    ]
    scratch = [
        *[pltpu.VMEM(leaf.shape, leaf.dtype) for leaf in large],
        bf(1024, 1024), bf(256, 1024), bf(2, 1024, 384), bf(8, 4, 32, 1024), bf(1024, 1024),
        bf(1024, 1024), bf(1024, 1024), bf(16, 128), bf(3, 16, 128), bf(16, 1024), fl(16, 1024),
        fl(2, 1024, 256), bf(2, 1024, 384), fl(1024, 256), bf(1024, 256), bf(4, 256, 256),
        fl(256, 1024), fl(256, 1024), bf(1024, 1024), bf(1024, 1024), bf(1024, 1024), bf(1024, 1024),
        bf(1024, 1024), bf(3, 256, 1024), bf(3, 256, 1024), bf(3, 256, 1024),
        fl(256, 1024), fl(256, 1024), fl(256, 1024), bf(1024, 1024), bf(256, 1024), bf(3, 256, 256),
        bf(1024, 256), bf(2, 1024, 384), fl(4, 8, 256),
        bf(1024, 1024), bf(128, 512), bf(4, 128, 512), bf(4, 128, 1024), bf(4, 128, 1024),
        bf(2, 4, 128, 384), bf(4, 32, 1024), bf(4, 256, 512), bf(4, 128, 512), bf(4, 128, 1024), bf(4, 128, 1024), bf(2, 4, 128, 384),
        bf(4, 32, 1024), bf(256, 1024), bf(256, 1024), bf(256, 1024), bf(256, 1024),
        fl(2, 128, 384), bf(2, 128, 384), bf(4, 2, 32, 384), fl(8, 1024), fl(3, 8, 1024), fl(2, 8, 1024), fl(4, 8, 1024),
        pltpu.SemaphoreType.DMA((COPIES,)), pltpu.SemaphoreType.DMA((COPIES,)),
        pltpu.SemaphoreType.DMA((32,)),
    ]
    *big, stats = pl.pallas_call(
        fused_kernel,
        out_shape=[*large, jax.ShapeDtypeStruct((8, 1024), F32)],
        in_specs=[hbm, hbm, smem, hbm, hbm, vmem, vmem, vmem, hbm, hbm, hbm, vmem, vmem],
        out_specs=[*[hbm] * 7, vmem],
        scratch_shapes=scratch,
        compiler_params=pltpu.CompilerParams(
            collective_id=0, has_side_effects=True, vmem_limit_bytes=VMEM_BYTES
        ),
        cost_estimate=pl.CostEstimate(
            flops=27_000_000_000, bytes_accessed=8_000_000, transcendentals=10_000_000
        ),
    )(
        tokens, cotangent, bucket_start, w_qkv, w_out, s_qk, alpha_a, alpha_m,
        w_up, w_gate, w_down, s_u, s_v,
    )
    entries = n_rows * width * lax.axis_size("dp") * lax.axis_size("tensor")
    flat = [(piece,), (piece,), (piece,), (1024,), (1024,), (3,)]
    *big, g_qk, g_a, g_m, g_u, g_v, stream = pl.pallas_call(
        functools.partial(finish_kernel, float(entries)),
        out_shape=[*large, *[jax.ShapeDtypeStruct(shape, F32) for shape in flat]],
        in_specs=[hbm] * 7 + [vmem],
        out_specs=[hbm] * 7 + [vmem] * 6,
        scratch_shapes=[
            *[pltpu.VMEM(leaf.shape, leaf.dtype) for leaf in large],
            pltpu.SemaphoreType.DMA((2, 7)),
        ],
    )(*big, stats)
    return (*big[:4], g_qk, g_a, g_m, *big[4:], g_u, g_v, stream)


def solution(mesh):
    body = fused if fits(mesh) else local
    return jax.shard_map(
        body,
        mesh=mesh,
        in_specs=(
            P(("dp", "tensor"), None),
            P(("dp", "tensor"), None),
            P(),
            P(("dp", "tensor"), None),
            P(("dp", "tensor"), None),
            P(("dp", "tensor")),
            P(("dp", "tensor")),
            P(("dp", "tensor")),
            P("dp", "tensor"),
            P("dp", "tensor"),
            P("dp", "tensor"),
            P("tensor"),
            P("tensor"),
        ),
        out_specs=(
            P(("dp", "tensor"), None),
            P(("dp", "tensor"), None),
            P(("dp", "tensor"), None),
            P(("dp", "tensor"), None),
            P(("dp", "tensor")),
            P(("dp", "tensor")),
            P(("dp", "tensor")),
            P("dp", "tensor"),
            P("dp", "tensor"),
            P("dp", "tensor"),
            P("tensor"),
            P("tensor"),
            P(),
        ),
        check_vma=False,
    )
```

profile of v0, /device:TPU:0, one launch (start us, length us, event | category | flops | bytes accessed | tf_op | source)
XLA Modules:
  0.0 232.9 jit_solution(6731458249478131821)
XLA Ops:
  0.6 227.9 %shard_map.228 = (bf16[256,1024]{1,0:T(8,128)(2,1)}, bf16[256,1024]{1,0:T(8,128)(2,1)}, f32[32,3072]{1,0:T(8,128)}, f32[32,1024]{1,0:T(8,128)}, f32[128,1024]{1,...) custom-call(bf16[256,1024]{1,0:T(8,128)(2,1)} %tokens.1, bf16[256,1024]{1,0:T(8,128)(2,1)} %cotangent.1, ...), custom_call_target="tpu_custom_call" | custom-call | flops 27000000512 | bytes 8000000 | tf_op jit(solution)/shard_map/pallas_call | solution.py:1411
  228.5 4.2 %shard_map.229 = (bf16[256,1024]{1,0:T(8,128)(2,1)}, bf16[256,1024]{1,0:T(8,128)(2,1)}, f32[32,3072]{1,0:T(8,128)}, f32[32,1024]{1,0:T(8,128)}, f32[128,1024]{1,...) custom-call(bf16[256,1024]{1,0:T(8,128)(2,1)} %get-tuple-element.34., ...), custom_call_target="tpu_custom_call" | custom-call | tf_op jit(solution)/shard_map/pallas_call | solution.py:1429
where the time goes:
time: 233 us
  Pallas kernels  232 us (100%)
    pallas_call x1, Pallas kernels, fused(): pl.pallas_call(fused_kernel, out_shape=[*large, jax.ShapeDtypeStruct((8,...  228 us

commit v1 on v0

--- a/solution.py
+++ b/solution.py
@@ -389,8 +389,8 @@
 def fused_kernel(
     tokens, cotangent, bucket_start, w_qkv, w_out, s_qk, alpha_a, alpha_m, w_up, w_gate, w_down, scale_u,
     scale_v,
-    layer_hbm, tokens_hbm, qkv_hbm, out_hbm, up_hbm, gate_hbm, down_hbm, stats_out,
-    layer_out, grad_tokens, grad_qkv, grad_out, grad_up, grad_gate, grad_down,
+    layer_hbm, tokens_hbm, qkv_hbm, out_hbm, up_hbm, gate_hbm, down_hbm, stats_hbm,
+    layer_out, grad_tokens, grad_qkv, grad_out, grad_up, grad_gate, grad_down, stats_sum,
     tok, cot, wq, wo, wu, wg, wd, small, small_t, small_d, gains,
     raw, qkv, linv, att, ato, branch, hid, h1, ur, gr, inn,
     part, from_core3, from_core1, from_y,
@@ -822,16 +822,20 @@
                 self.copies[3] = send(part.at[block(3)], from_core3.at[k], core)
             elif r == 2:
                 self.copies[3].wait_recv()
-                part[block(2), :] = (
-                    part[block(2), :].astype(F32) + from_core3[k].astype(F32)
-                ).astype(BF16)
-                self.copies[2] = send(part.at[block(2)], from_y.at[k], ynb)
+                self.copies[2] = []
+                for c in range(4):
+                    here, there = pl.ds(512 + c * 64, 64), pl.ds(c * 64, 64)
+                    part[here, :] = (
+                        part[here, :].astype(F32) + from_core3[k, there, :].astype(F32)
+                    ).astype(BF16)
+                    self.copies[2].append(send(part.at[here], from_y.at[k, there], ynb))
             elif r == 1:
                 self.copies[1] = send(part.at[block(1)], from_core1.at[k], core)
 
         def finish(self):
             self.copies[1].wait_recv()
-            self.copies[2].wait_recv()
+            for copy in self.copies[2]:
+                copy.wait_recv()
 
         def at(self, where):
             k = self.which
@@ -853,19 +857,26 @@
             self.copies[3].append(send(part.at[block(3), cols], from_core3.at[0, :, cols], core))
             self.copies[1].append(send(part.at[block(1), cols], from_core1.at[0, :, cols], core))
 
-        def pass_on(self):
+        def pass_on(self, parts=1):
             done = len(self.copies[2])
             cols = self.columns[done]
             self.copies[3][done].wait_recv()
-            part[block(2), cols] = (
-                part[block(2), cols].astype(F32) + from_core3[0, :, cols].astype(F32)
-            ).astype(BF16)
-            self.copies[2].append(send(part.at[block(2), cols], from_y.at[0, :, cols], ynb))
+            count = 256 // parts
+            for c in range(parts):
+                here, there = pl.ds(512 + c * count, count), pl.ds(c * count, count)
+                part[here, cols] = (
+                    part[here, cols].astype(F32) + from_core3[0, there, cols].astype(F32)
+                ).astype(BF16)
+                self.copies[2].append(
+                    send(part.at[here, cols], from_y.at[0, there, cols], ynb)
+                )
 
         def finish(self):
-            for r in (1, 2):
-                for copy in self.copies[r]:
-                    copy.wait_recv()
+            for copy in self.copies[1] + self.copies[2][:-4]:
+                copy.wait_recv()
+
+        def finish_rows(self, c):
+            self.copies[2][c - 4].wait_recv()
 
         at = Reduce.at
         which = 0
@@ -880,7 +891,7 @@
     take_down.straight.wait_recv()
     sum_m.step(3)
     sum_m.pass_on()
-    sum_m.pass_on()
+    sum_m.pass_on(4)
     sum_m.finish()
 
     def loss_step(c, carry):
@@ -920,6 +931,7 @@
 
     db_rows = Spread(db)
     for c in range(4):
+        sum_m.finish_rows(c)
         lax.fori_loop(c * (64 // CH), (c + 1) * (64 // CH), loss_step, 0)
         db_rows.start(c)
 
@@ -1042,6 +1054,7 @@
         lax.fori_loop(0, 256 // CH, inner_step, 0)
         part[at, :] = (nt(ur[at, :], wu[...]) + nt(gr[at, :], wg[...])).astype(BF16)
 
+    forward_sends = len(issued)
     sum_h = Reduce(1, sum_m, make_hidden)
     for copy in db_rows.core[:4]:
         copy.wait_recv()
@@ -1079,7 +1092,6 @@
     weight_grad(h1, gr, gg, sum_gate)
     sum_down_x.fold(3)
     sum_down_x.fold(1)
-    sum_h.finish()
 
     def mid_step(c, carry):
         at = rows(c, CH)
@@ -1092,7 +1104,10 @@
         dba[at, :] = (fa * (c_a - ha * mean_rows(c_a * ha))).astype(BF16)
         return carry
 
-    lax.fori_loop(0, 256 // CH, mid_step, 0)
+    sum_h.copies[1].wait_recv()
+    for c in range(4):
+        sum_h.copies[2][c].wait_recv()
+        lax.fori_loop(c * (64 // CH), (c + 1) * (64 // CH), mid_step, 0)
 
     dat_sends = []
     for r in (2, 3, 1, 0):
@@ -1289,6 +1304,10 @@
         outgoing.append(bring(src, dst))
 
     put(layer_out, layer_hbm)
+    for gather in (take_qkv, take_small, take_out):
+        gather.release()
+    for copy in issued[:forward_sends]:
+        sent(copy)
     down_x.wait_recv()
     grad_down[:, half[0]] = gd[rows(d, 128), half[0]].astype(F32) + x_down[...].astype(F32)
     sum_down_x.total_into(grad_down.at[:, half[1]])
@@ -1320,7 +1339,8 @@
     put(grad_tokens, tokens_hbm)
     for copy in stat_z:
         copy.wait_recv()
-    stats_out[...] = s_z[0] + s_z[1] + s_z[2] + s_z[3]
+    stats_sum[...] = s_z[0] + s_z[1] + s_z[2] + s_z[3]
+    put(stats_sum, stats_hbm)
     for copy in q_sends:
         copy.wait_recv()
     for slot in range(4):
@@ -1330,8 +1350,6 @@
                 slot, pair, :, j * 128 : j * 128 + 128
             ].astype(F32)
     put(grad_qkv, qkv_hbm)
-    for gather in (take_qkv, take_small, take_out):
-        gather.release()
     for scatter in (sum_down, sum_down_x, sum_up, sum_gate, sum_out, *sum_qkv):
         scatter.settle()
     for copy in issued:
@@ -1341,17 +1359,22 @@
 
 
 def finish_kernel(entries, *refs):
-    large, stats, outs, held, sems = refs[:7], refs[7], refs[8:21], refs[21:28], refs[28]
-    taken = [pltpu.make_async_copy(large[i], held[i], sems.at[0, i]) for i in range(7)]
-    given = [pltpu.make_async_copy(held[i], outs[i], sems.at[1, i]) for i in range(7)]
-    for copy in taken:
+    taken, given, held, sems = refs[:8], refs[8:21], refs[21:35], refs[35]
+    pull = [pltpu.make_async_copy(taken[i], held[i], sems.at[i]) for i in range(8)]
+    push = [
+        pltpu.make_async_copy(held[i if i < 7 else i + 1], given[i], sems.at[8 + i])
+        for i in range(13)
+    ]
+    for copy in (pull[7], *pull[:7]):
         copy.start()
-    s_qk, alpha_a, alpha_m, s_u, s_v, stream = outs[7:]
+    stats, outs = held[7], held[8:]
+    s_qk, alpha_a, alpha_m, s_u, s_v, stream = outs
     index = lax.axis_index("dp") * lax.axis_size("tensor") + lax.axis_index("tensor")
     piece = s_qk.shape[0]
     pick = lax.broadcasted_iota(jnp.int32, (1024, piece), 0) == (
         lax.broadcasted_iota(jnp.int32, (1024, piece), 1) + index * piece
     )
+    pull[7].wait()
     own = lax.dot_general(
         stats[0:3, :],
         jnp.where(pick, 1.0, 0.0),
@@ -1364,10 +1387,12 @@
     s_u[...] = stats[6, :]
     s_v[...] = stats[7, :]
     stream[...] = jnp.sqrt(jnp.sum(stats[3:6, :], axis=1) / entries)
+    for copy in push[7:]:
+        copy.start()
     for i in range(7):
-        taken[i].wait()
-        given[i].start()
-    for copy in given:
+        pull[i].wait()
+        push[i].start()
+    for copy in push:
         copy.wait()
 
 
@@ -1393,7 +1418,7 @@
         )
     ]
     scratch = [
-        *[pltpu.VMEM(leaf.shape, leaf.dtype) for leaf in large],
+        *[pltpu.VMEM(leaf.shape, leaf.dtype) for leaf in large], fl(8, 1024),
         bf(1024, 1024), bf(256, 1024), bf(2, 1024, 384), bf(8, 4, 32, 1024), bf(1024, 1024),
         bf(1024, 1024), bf(1024, 1024), bf(16, 128), bf(3, 16, 128), bf(16, 1024), fl(16, 1024),
         fl(2, 1024, 256), bf(2, 1024, 384), fl(1024, 256), bf(1024, 256), bf(4, 256, 256),
@@ -1412,7 +1437,7 @@
         fused_kernel,
         out_shape=[*large, jax.ShapeDtypeStruct((8, 1024), F32)],
         in_specs=[hbm, hbm, smem, hbm, hbm, vmem, vmem, vmem, hbm, hbm, hbm, vmem, vmem],
-        out_specs=[*[hbm] * 7, vmem],
+        out_specs=[hbm] * 8,
         scratch_shapes=scratch,
         compiler_params=pltpu.CompilerParams(
             collective_id=0, has_side_effects=True, vmem_limit_bytes=VMEM_BYTES
@@ -1429,11 +1454,13 @@
     *big, g_qk, g_a, g_m, g_u, g_v, stream = pl.pallas_call(
         functools.partial(finish_kernel, float(entries)),
         out_shape=[*large, *[jax.ShapeDtypeStruct(shape, F32) for shape in flat]],
-        in_specs=[hbm] * 7 + [vmem],
-        out_specs=[hbm] * 7 + [vmem] * 6,
+        in_specs=[hbm] * 8,
+        out_specs=[hbm] * 13,
         scratch_shapes=[
             *[pltpu.VMEM(leaf.shape, leaf.dtype) for leaf in large],
-            pltpu.SemaphoreType.DMA((2, 7)),
+            fl(8, 1024),
+            *[fl(*shape) for shape in flat],
+            pltpu.SemaphoreType.DMA((21,)),
         ],
     )(*big, stats)
     return (*big[:4], g_qk, g_a, g_m, *big[4:], g_u, g_v, stream)

time: 233 us -> 229 us (0.983)
  Pallas kernels: 232 us -> 228 us
    pallas_call x1, Pallas kernels: 228 us -> 225 us  [fused(): pl.pallas_call(fused_kernel, out_shape=[*large, jax.ShapeDtypeStruct((8,...]
where the time goes in v1:
time: 229 us
  Pallas kernels  228 us (100%)
    pallas_call x1, Pallas kernels, fused(): pl.pallas_call(fused_kernel, out_shape=[*large, jax.ShapeDtypeStruct((8,...  225 us

profile of v1, /device:TPU:0, one launch (start us, length us, event | category | flops | bytes accessed | tf_op | source)
XLA Modules:
  0.0 229.0 jit_solution(5797763778682101100)
XLA Ops:
  0.6 225.2 %shard_map.228 = (bf16[256,1024]{1,0:T(8,128)(2,1)}, bf16[256,1024]{1,0:T(8,128)(2,1)}, f32[32,3072]{1,0:T(8,128)}, f32[32,1024]{1,0:T(8,128)}, f32[128,1024]{1,...) custom-call(bf16[256,1024]{1,0:T(8,128)(2,1)} %tokens.1, bf16[256,1024]{1,0:T(8,128)(2,1)} %cotangent.1, ...), custom_call_target="tpu_custom_call" | custom-call | flops 27000000512 | bytes 8000000 | tf_op jit(solution)/shard_map/pallas_call | solution.py:1436
  225.8 3.0 %shard_map.229 = (bf16[256,1024]{1,0:T(8,128)(2,1)}, bf16[256,1024]{1,0:T(8,128)(2,1)}, f32[32,3072]{1,0:T(8,128)}, f32[32,1024]{1,0:T(8,128)}, f32[128,1024]{1,...) custom-call(bf16[256,1024]{1,0:T(8,128)(2,1)} %get-tuple-element.34., ...), custom_call_target="tpu_custom_call" | custom-call | tf_op jit(solution)/shard_map/pallas_call | solution.py:1454

commit v2 on v1

--- a/solution.py
+++ b/solution.py
@@ -387,10 +387,11 @@
 
 
 def fused_kernel(
-    tokens, cotangent, bucket_start, w_qkv, w_out, s_qk, alpha_a, alpha_m, w_up, w_gate, w_down, scale_u,
-    scale_v,
+    tokens, cotangent, starts_hbm, w_qkv, w_out, s_qk_hbm, alpha_a_hbm, alpha_m_hbm, w_up, w_gate,
+    w_down, scale_u_hbm, scale_v_hbm,
     layer_hbm, tokens_hbm, qkv_hbm, out_hbm, up_hbm, gate_hbm, down_hbm, stats_hbm,
     layer_out, grad_tokens, grad_qkv, grad_out, grad_up, grad_gate, grad_down, stats_sum,
+    bucket_start, s_qk, alpha_a, alpha_m, scale_u, scale_v,
     tok, cot, wq, wo, wu, wg, wd, small, small_t, small_d, gains,
     raw, qkv, linv, att, ato, branch, hid, h1, ur, gr, inn,
     part, from_core3, from_core1, from_y,
@@ -541,6 +542,17 @@
     take_gate = Gather(w_gate, rows_of(wg))
     take_down = GatherPairs(w_down, rows_of(wd), pair_of(wd))
 
+    local_small = [
+        bring(src, dst)
+        for src, dst in (
+            (s_qk_hbm, s_qk),
+            (alpha_a_hbm, alpha_a),
+            (alpha_m_hbm, alpha_m),
+            (scale_u_hbm, scale_u),
+            (scale_v_hbm, scale_v),
+            (starts_hbm, bucket_start),
+        )
+    ]
     piece = s_qk.shape[0]
     own_qkv = pl.ds(pl.multiple_of(d * 128 + t * 32, 32), 32)
 
@@ -569,6 +581,8 @@
         0.0,
     ).astype(BF16)
     small_row = lax.broadcasted_iota(jnp.int32, (16, 128), 0)
+    for copy in local_small:
+        copy.wait()
     placed = jnp.zeros((16, 128), F32)
     for index, vector in enumerate((s_qk, alpha_a, alpha_m)):
         placed = jnp.where(small_row == index, nn(vector[...].reshape(1, piece), place), placed)
@@ -1252,6 +1266,14 @@
     qkv_back(0)
     qkv_weight(0)
     clear()
+    sum_gate.fold(3)
+    sum_gate.fold(1)
+    lax.fori_loop(0, 4, diagonal(1), 0)
+    sum_gate.fold(2)
+    sum_gate.push(2)
+    lax.fori_loop(0, 6, below(1), 0)
+    qkv_back(1)
+    qkv_weight(1)
     go_core1.wait_recv()
     go_y.wait_recv()
     osum[...] = (
@@ -1260,14 +1282,6 @@
     sum_out = Scatter(rows_of(osum, 32), x_out, z_out)
     for k in (3, 1, 2, 0):
         sum_out.ship(k)
-    sum_gate.fold(3)
-    sum_gate.fold(1)
-    lax.fori_loop(0, 4, diagonal(1), 0)
-    sum_gate.fold(2)
-    sum_gate.push(2)
-    lax.fori_loop(0, 6, below(1), 0)
-    qkv_back(1)
-    qkv_weight(1)
     sum_gate.fold(0)
     sum_down.total_into(down_pair(d))
     down_x = send(gd.at[rows(flip(d, 1), 128), half[0]], x_down, xnb)
@@ -1285,9 +1299,6 @@
         sum_qkv[0].fold(k)
     sum_t.run((1, 0))
     sum_qkv[0].push(2)
-    for k in (3, 1, 2, 0):
-        sum_out.fold(k)
-    sum_out.push(2)
     for copy in small_back:
         copy.wait_recv()
     over_tensor = s_tensor[0] + s_tensor[1] + s_tensor[2]
@@ -1297,6 +1308,9 @@
     for k in (3, 1, 0, 2):
         sum_qkv[1].fold(k)
     sum_qkv[1].push(2)
+    for k in (3, 1, 2, 0):
+        sum_out.fold(k)
+    sum_out.push(2)
 
     outgoing = []
 
@@ -1308,16 +1322,11 @@
         gather.release()
     for copy in issued[:forward_sends]:
         sent(copy)
-    down_x.wait_recv()
-    grad_down[:, half[0]] = gd[rows(d, 128), half[0]].astype(F32) + x_down[...].astype(F32)
     sum_down_x.total_into(grad_down.at[:, half[1]])
-    put(grad_down, down_hbm)
     sum_up.total_into(grad_up)
     put(grad_up, up_hbm)
     sum_gate.total_into(grad_gate)
     put(grad_gate, gate_hbm)
-    sum_out.total_into(grad_out)
-    put(grad_out, out_hbm)
     stat_x.wait_recv()
     s_z[0] = s_x[0] + s_x[1]
     stat_z = [send(s_z.at[0], s_z.at[k], z_peer[2 * k]) for k in (1, 2, 3)]
@@ -1337,6 +1346,11 @@
 
     lax.fori_loop(0, 256 // CH, last_step, 0)
     put(grad_tokens, tokens_hbm)
+    sum_out.total_into(grad_out)
+    put(grad_out, out_hbm)
+    down_x.wait_recv()
+    grad_down[:, half[0]] = gd[rows(d, 128), half[0]].astype(F32) + x_down[...].astype(F32)
+    put(grad_down, down_hbm)
     for copy in stat_z:
         copy.wait_recv()
     stats_sum[...] = s_z[0] + s_z[1] + s_z[2] + s_z[3]
@@ -1405,8 +1419,6 @@
 ):
     n_rows, width = tokens.shape
     piece = s_qk.shape[0]
-    vmem = pl.BlockSpec(memory_space=pltpu.VMEM)
-    smem = pl.BlockSpec(memory_space=pltpu.SMEM)
     hbm = pl.BlockSpec(memory_space=pl.ANY)
     bf = lambda *shape: pltpu.VMEM(shape, BF16)
     fl = lambda *shape: pltpu.VMEM(shape, F32)
@@ -1417,8 +1429,11 @@
             ((128, 1024), F32), ((128, 1024), F32), ((128, 1024), F32),
         )
     ]
+    vector = lambda leaf: pltpu.VMEM(leaf.shape, leaf.dtype)
     scratch = [
         *[pltpu.VMEM(leaf.shape, leaf.dtype) for leaf in large], fl(8, 1024),
+        pltpu.SMEM(bucket_start.shape, jnp.int32), vector(s_qk), vector(alpha_a), vector(alpha_m),
+        vector(s_u), vector(s_v),
         bf(1024, 1024), bf(256, 1024), bf(2, 1024, 384), bf(8, 4, 32, 1024), bf(1024, 1024),
         bf(1024, 1024), bf(1024, 1024), bf(16, 128), bf(3, 16, 128), bf(16, 1024), fl(16, 1024),
         fl(2, 1024, 256), bf(2, 1024, 384), fl(1024, 256), bf(1024, 256), bf(4, 256, 256),
@@ -1436,7 +1451,7 @@
     *big, stats = pl.pallas_call(
         fused_kernel,
         out_shape=[*large, jax.ShapeDtypeStruct((8, 1024), F32)],
-        in_specs=[hbm, hbm, smem, hbm, hbm, vmem, vmem, vmem, hbm, hbm, hbm, vmem, vmem],
+        in_specs=[hbm] * 13,
         out_specs=[hbm] * 8,
         scratch_shapes=scratch,
         compiler_params=pltpu.CompilerParams(

time: 229 us -> 226 us (0.987)
  Pallas kernels: 228 us -> 225 us
    pallas_call x1, Pallas kernels: 225 us -> 222 us  [fused(): pl.pallas_call(fused_kernel, out_shape=[*large, jax.ShapeDtypeStruct((8,...]
where the time goes in v2:
time: 226 us
  Pallas kernels  225 us (100%)
    pallas_call x1, Pallas kernels, fused(): pl.pallas_call(fused_kernel, out_shape=[*large, jax.ShapeDtypeStruct((8,...  222 us

profile of v2, /device:TPU:0, one launch (start us, length us, event | category | flops | bytes accessed | tf_op | source)
XLA Modules:
  0.0 225.6 jit_solution(15283315817837391228)
XLA Ops:
  0.6 221.8 %shard_map.228 = (bf16[256,1024]{1,0:T(8,128)(2,1)}, bf16[256,1024]{1,0:T(8,128)(2,1)}, f32[32,3072]{1,0:T(8,128)}, f32[32,1024]{1,0:T(8,128)}, f32[128,1024]{1,...) custom-call(bf16[256,1024]{1,0:T(8,128)(2,1)} %tokens.1, bf16[256,1024]{1,0:T(8,128)(2,1)} %cotangent.1, ...), custom_call_target="tpu_custom_call" | custom-call | flops 27000000512 | bytes 8000000 | tf_op jit(solution)/shard_map/pallas_call | solution.py:1451
  222.4 3.0 %shard_map.229 = (bf16[256,1024]{1,0:T(8,128)(2,1)}, bf16[256,1024]{1,0:T(8,128)(2,1)}, f32[32,3072]{1,0:T(8,128)}, f32[32,1024]{1,0:T(8,128)}, f32[128,1024]{1,...) custom-call(bf16[256,1024]{1,0:T(8,128)(2,1)} %get-tuple-element.34., ...), custom_call_target="tpu_custom_call" | custom-call | tf_op jit(solution)/shard_map/pallas_call | solution.py:1469
